TPU v7x, 32 devices: a whole 2x2x4 slice. The times are simulated.
32 devices in a mesh: grp: 4 (over y, core), tile: 8 (over z, x).
Axes of the slice: x: 2, y: 2, z: 4, core: 2. Of those that a mesh axis runs over, the one named last changes fastest.
Arguments:
- adjoint_state: float32 [64, 128, 2048], P('tile', 'grp'), may hold values from -6 to 6
- misfit: float32 [64, 128, 2048], P('tile', 'grp'), may hold values from -4 to 4
- east_speed: float32 [64, 128, 2048], P('tile', 'grp'), may hold values from -0.6 to 0.6
- north_speed: float32 [64, 128, 2048], P('tile', 'grp'), may hold values from -0.6 to 0.6
- land_mask: int32 [64, 128, 2048], P('tile', 'grp'), may hold values 0 or 1
- warming_forcing_selector: int32 [128, 2048], P('grp', 'tile'), may hold values 0 or 1
- vertical_filter_matrix: float32 [64, 64], replicated, may hold values from 0 to 0.54
Outputs:
- filtered_thermal_sensitivity: float32 [64, 128, 2048], P('tile', 'grp')
- boundary_warming_sensitivity: float32 [128, 2048], P('grp', 'tile')
All inputs are finite; a program needn't handle non-finite values. No bound on the sum of `land_mask` or of `warming_forcing_selector` on one device may be relied on, other than what follows from the above.
Results may differ from a plain program's by a relative error of at most 0.000088.
Values sent between devices are 32-bit elements; how exact they have to be, the bound alone decides.
A program may use at most 192 MiB of HBM per device.

v0:
```python
import jax
import jax.numpy as jnp
from jax import lax
from jax.sharding import PartitionSpec as P

STEPS = 2


def with_halo(cells, sides, width):
    for axis, dim in sides:
        count = lax.axis_size(axis)
        ends = count - 1
        head = lax.slice_in_dim(cells, 0, width, axis=dim)
        tail = lax.slice_in_dim(cells, cells.shape[dim] - width, cells.shape[dim], axis=dim)
        cells = jnp.concatenate(
            [
                lax.ppermute(tail, axis, [(i, (i + 1) % count) for i in range(ends)]),
                cells,
                lax.ppermute(head, axis, [((i + 1) % count, i) for i in range(ends)]),
            ],
            axis=dim,
        )
    return cells


def advance(padded, misfit, east_speed, north_speed, wet_cells):
    center = padded[1:-1, 1:-1, 1:-1]
    east_cell = padded[1:-1, 1:-1, 2:]
    western_neighbour = padded[1:-1, 1:-1, :-2]
    north_cell = padded[1:-1, 2:, 1:-1]
    south_cell = padded[1:-1, :-2, 1:-1]
    upper_cell = padded[:-2, 1:-1, 1:-1]
    lower_cell = padded[2:, 1:-1, 1:-1]
    vertical = upper_cell + lower_cell - 2.0 * center
    lateral = east_cell + western_neighbour + north_cell + south_cell - 4.0 * center
    change = 0.5 * east_speed * (east_cell - western_neighbour) + 0.5 * north_speed * (
        north_cell - south_cell
    )
    return wet_cells * (center + misfit + change + 0.1 * lateral + 0.15 * vertical)


def smooth_levels(vertical_filter_matrix, pencil):
    return jnp.einsum(
        "cz,zne->cne", vertical_filter_matrix, pencil, precision=lax.Precision.HIGHEST
    )


def body(
    adjoint_state,
    misfit,
    east_speed,
    north_speed,
    land_mask,
    warming_forcing_selector,
    vertical_filter_matrix,
):
    wet_cells = land_mask.astype(jnp.float32)
    current_tracer_values = adjoint_state
    for step_index in range(STEPS):
        bordered = with_halo(current_tracer_values, (("grp", 1), ("tile", 0)), 1)
        padded = jnp.pad(bordered, ((0, 0), (0, 0), (1, 1)))
        current_tracer_values = advance(padded, misfit, east_speed, north_speed, wet_cells)
    pencil = lax.all_to_all(current_tracer_values, "tile", split_axis=2, concat_axis=0, tiled=True)
    smoothed_field = smooth_levels(vertical_filter_matrix, pencil)
    surface_layer = smoothed_field[0]
    filtered_thermal_sensitivity = lax.all_to_all(
        smoothed_field, "tile", split_axis=0, concat_axis=2, tiled=True
    )
    boundary_warming_sensitivity = warming_forcing_selector.astype(jnp.float32) * surface_layer
    return (filtered_thermal_sensitivity, boundary_warming_sensitivity)


def solution(mesh):
    in_specs = (
        P("tile", "grp", None),
        P("tile", "grp", None),
        P("tile", "grp", None),
        P("tile", "grp", None),
        P("tile", "grp", None),
        P("grp", "tile"),
        P(),
    )
    out_specs = (P("tile", "grp", None), P("grp", "tile"))
    return jax.shard_map(body, mesh=mesh, in_specs=in_specs, out_specs=out_specs, check_vma=False)
```

profile of v0, /device:TPU:0, one launch (start us, length us, event | category | flops | bytes accessed | tf_op | source)
XLA Modules:
  0.0 217.6 jit_solution(6359021577452492257)
XLA Ops:
  0.6 0.0 copy-start
  0.6 0.0 copy-start.1
  0.7 1.4 fusion.18
  2.1 2.4 %collective-permute-start = (f32[8,1,2048]{2,0,1:T(8,128)S(1)}, f32[8,1,2048]{2,0,1:T(8,128)S(1)}, u32[]{:S(2)}, u32[]{:S(2)}) collective-permute-start(f32[8,1,2048]{2,0,1:T(8,128)S(1)} %copy.101), channel_id=1, source_target_pairs={{0,8},{8,16},{16,24},{1,9},{9,17},{17,25},{2,10},{10,18},{18,26},{... | collective-permute-start | bytes 196616 | tf_op jit(solution)/shard_map/ppermute | solution.py:17
  4.5 1.3 collective-permute-start.1
  5.8 0.0 collective-permute-done
  5.8 0.1 copy.86
  5.9 3.9 %collective-permute-done.1 = f32[8,1,2048]{2,0,1:T(8,128)S(1)} collective-permute-done((f32[8,1,2048]{2,0,1:T(8,128)S(1)}, f32[8,1,2048]{2,0,1:T(8,128)S(1)}, u32[]{:S(2)}, u32[]{:S(2)}) %collective-permute-start.1) | collective-permute-done | bytes 65568 | tf_op jit(solution)/shard_map/ppermute | solution.py:19
  9.8 0.1 copy.87
  9.9 1.1 pad_maximum_fusion.21
  11.0 3.4 %collective-permute-start.2 = (f32[1,34,2048]{2,1,0:T(8,128)S(1)}, f32[1,34,2048]{2,1,0:T(8,128)S(1)}, u32[]{:S(2)}, u32[]{:S(2)}) collective-permute-start(f32[1,34,2048]{2,1,0:T(8,128)S(1)} %get-tuple-element.4), channel_id=1, source_target_pairs={{0,1},{1,2},{2,3},{3,4},{4,5},{5,6},{6,7},{8,9},{9,10},{10,11},{11... | collective-permute-start | bytes 835592 | tf_op jit(solution)/shard_map/ppermute | solution.py:17
  14.4 0.0 copy-start.2
  14.4 0.0 copy-start.3
  14.5 0.0 copy-start.4
  14.5 1.6 collective-permute-start.3
  16.0 4.3 %collective-permute-done.2 = f32[1,34,2048]{2,1,0:T(8,128)S(1)} collective-permute-done((f32[1,34,2048]{2,1,0:T(8,128)S(1)}, f32[1,34,2048]{2,1,0:T(8,128)S(1)}, u32[]{:S(2)}, u32[]{:S(2)}) %collective-permute-start.2) | collective-permute-done | bytes 278560 | tf_op jit(solution)/shard_map/ppermute | solution.py:17
  20.3 5.0 %collective-permute-done.3 = f32[1,34,2048]{2,1,0:T(8,128)S(1)} collective-permute-done((f32[1,34,2048]{2,1,0:T(8,128)S(1)}, f32[1,34,2048]{2,1,0:T(8,128)S(1)}, u32[]{:S(2)}, u32[]{:S(2)}) %collective-permute-start.3) | collective-permute-done | bytes 278560 | tf_op jit(solution)/shard_map/ppermute | solution.py:19
  25.3 3.1 %select_maximum_fusion.4 = f32[10,34,2050]{2,1,0:T(8,128)S(1)} fusion(f32[1,34,2048]{2,1,0:T(8,128)S(1)} %collective-permute-done.3, f32[1,34,2048]{2,1,0:T(8,128)S(1)} %collective-permute-done.2, f32[8,1,2048]{2,1,0:T(1,128)S(1)} %copy.87, f32[8,32,2048]{2,1,0:T(8,128)S(1)} %copy-done.1, f32[8,1,2048]{2,1,0:T(1,128)S(1)} %copy.86), kind=kLoop, calls=%fused_computation.6 | loop fusion | flops 8364000 | bytes 5573280 | tf_op jit(solution)/shard_map/concatenate | solution.py:15
  28.5 4.3 %fusion.10 = f32[8,32,2048]{2,1,0:T(8,128)S(1)} fusion(f32[1,34,2048]{2,1,0:T(8,128)S(1)} %collective-permute-done.3, f32[8,1,2048]{2,1,0:T(1,128)S(1)} %copy.87, f32[8,32,2048]{2,1,0:T(8,128)S(1)} %copy-done.1, f32[8,1,2048]{2,1,0:T(1,128)S(1)} %copy.86, f32[1,34,2048]{2,1,0:T(8,128)S(1)} %collective-permute-done.2, ...), kind=kLoop, calls=%fused_computation.29 | loop fusion | flops 16252928 | bytes 17465344 | tf_op jit(solution)/shard_map/mul | solution.py:39
  32.8 0.1 fusion.17
  32.9 6.2 %collective-permute-start.4 = (f32[8,1,2048]{2,0,1:T(8,128)S(1)}, f32[8,1,2048]{2,0,1:T(8,128)S(1)}, u32[]{:S(2)}, u32[]{:S(2)}) collective-permute-start(f32[8,1,2048]{2,0,1:T(8,128)S(1)} %copy.90), channel_id=1, source_target_pairs={{0,8},{8,16},{16,24},{1,9},{9,17},{17,25},{2,10},{10,18},{18,26},{... | collective-permute-start | bytes 196616 | tf_op jit(solution)/shard_map/ppermute | solution.py:17
  39.1 1.3 collective-permute-start.5
  40.4 0.0 collective-permute-done.4
  40.5 0.1 copy.92
  40.5 1.8 collective-permute-done.5
  42.3 0.1 copy.93
  42.4 0.1 pad_maximum_fusion.18
  42.5 4.1 %collective-permute-start.6 = (f32[1,34,2048]{2,1,0:T(8,128)S(1)}, f32[1,34,2048]{2,1,0:T(8,128)S(1)}, u32[]{:S(2)}, u32[]{:S(2)}) collective-permute-start(f32[1,34,2048]{2,1,0:T(8,128)S(1)} %get-tuple-element.2), channel_id=1, source_target_pairs={{0,1},{1,2},{2,3},{3,4},{4,5},{5,6},{6,7},{8,9},{9,10},{10,11},{11... | collective-permute-start | bytes 835592 | tf_op jit(solution)/shard_map/ppermute | solution.py:17
  46.6 0.0 copy-start.5
  46.6 1.4 collective-permute-start.7
  48.0 5.1 %collective-permute-done.6 = f32[1,34,2048]{2,1,0:T(8,128)S(1)} collective-permute-done((f32[1,34,2048]{2,1,0:T(8,128)S(1)}, f32[1,34,2048]{2,1,0:T(8,128)S(1)}, u32[]{:S(2)}, u32[]{:S(2)}) %collective-permute-start.6) | collective-permute-done | bytes 278560 | tf_op jit(solution)/shard_map/ppermute | solution.py:17
  53.1 5.2 %collective-permute-done.7 = f32[1,34,2048]{2,1,0:T(8,128)S(1)} collective-permute-done((f32[1,34,2048]{2,1,0:T(8,128)S(1)}, f32[1,34,2048]{2,1,0:T(8,128)S(1)}, u32[]{:S(2)}, u32[]{:S(2)}) %collective-permute-start.7) | collective-permute-done | bytes 278560 | tf_op jit(solution)/shard_map/ppermute | solution.py:19
  58.3 3.1 %select_maximum_fusion = f32[10,34,2050]{2,1,0:T(8,128)S(1)} fusion(f32[1,34,2048]{2,1,0:T(8,128)S(1)} %collective-permute-done.7, f32[1,34,2048]{2,1,0:T(8,128)S(1)} %collective-permute-done.6, f32[8,1,2048]{2,1,0:T(1,128)S(1)} %copy.93, f32[8,32,2048]{2,1,0:T(8,128)S(1)} %fusion.10, f32[8,1,2048]{2,1,0:T(1,128)S(1)} %copy.92), kind=kLoop, calls=%fused_computation.2 | loop fusion | flops 8364000 | bytes 5573280 | tf_op jit(solution)/shard_map/concatenate | solution.py:15
  61.4 0.0 copy-done.5
  61.4 3.0 %fusion.5 = f32[8,32,2048]{2,1,0:T(8,128)S(1)} fusion(f32[1,34,2048]{2,1,0:T(8,128)S(1)} %collective-permute-done.7, f32[8,1,2048]{2,1,0:T(1,128)S(1)} %copy.93, f32[8,32,2048]{2,1,0:T(8,128)S(1)} %fusion.10, f32[8,1,2048]{2,1,0:T(1,128)S(1)} %copy.92, f32[1,34,2048]{2,1,0:T(8,128)S(1)} %collective-permute-done.6, ...), kind=kLoop, calls=%fused_computation.16 | loop fusion | flops 16252928 | bytes 17465344 | tf_op jit(solution)/shard_map/mul | solution.py:39
  64.5 4.7 %copy.96 = f32[8,32,2048]{1,0,2:T(8,128)} copy(f32[8,32,2048]{2,1,0:T(8,128)S(1)} %fusion.5) | data formatting | bytes 4194304 | tf_op jit(solution)/shard_map/mul | solution.py:39
  69.2 7.4 %reshape.5 = f32[8,1,65536]{2,1,0:T(1,128)S(1)} reshape(f32[2048,8,32]{2,1,0:T(8,128)} %bitcast.22) | data formatting | bytes 4194304
  76.6 59.5 %all_to_all.36 = f32[8,1,65536]{2,1,0:T(1,128)} all-to-all(f32[8,1,65536]{2,1,0:T(1,128)S(1)} %reshape.5), channel_id=1, replica_groups=mesh['grp'=4,'tile'=8] {'tile'}, dimensions={0} | all-to-all | bytes 4194304 | tf_op jit(solution)/shard_map/all_to_all | solution.py:63
  136.2 0.5 broadcast.70
  136.7 7.2 %reduce = f32[8,65536]{1,0:T(8,128)S(1)} reduce(f32[8,1,65536]{2,1,0:T(1,128)} %all_to_all.36, f32[]{:T(128)} %broadcast.70), dimensions={1}, to_apply=%all_to_all.26.reduce_sub_computation | reduce | bytes 4194308 | tf_op jit(solution)/shard_map/all_to_all | solution.py:63
  143.9 6.0 %reshape.6 = f32[2048,8,32]{2,1,0:T(8,128)} reshape(f32[8,65536]{1,0:T(8,128)S(1)} %reduce) | data formatting | bytes 4194304
  149.9 6.6 %copy.97 = f32[8,32,8,256]{3,0,2,1:T(8,128)} copy(f32[8,32,8,256]{1,0,3,2:T(8,128)} %bitcast.23) | data formatting | bytes 4194304 | tf_op jit(solution)/shard_map/all_to_all | solution.py:63
  156.5 3.6 %fusion.13 = f32[64,32,256]{2,0,1:T(8,128)S(1)} fusion(f32[8,32,8,256]{3,0,2,1:T(8,128)} %copy.97, f32[64,64]{1,0:T(8,128)S(1)} %copy-done), kind=kOutput, calls=%fused_computation.39 | convolution fusion | flops 402653184 | bytes 4210688 | tf_op jit(solution)/shard_map/cz,zne->cne/dot_general | solution.py:43
  160.1 2.5 %copy.98 = f32[64,32,256]{2,1,0:T(8,128)} copy(f32[64,32,256]{2,0,1:T(8,128)S(1)} %fusion.13) | data formatting | bytes 4194304 | tf_op jit(solution)/shard_map/cz,zne->cne/dot_general | solution.py:43
  162.6 4.5 %all-to-all-start.1 = ((f32[64,32,256]{2,1,0:T(8,128)}), f32[64,32,256]{2,1,0:T(8,128)}, u32[]{:S(2)}, u32[]{:S(2)}) async-start(f32[64,32,256]{2,1,0:T(8,128)} %copy.98), calls=%async_computation.1 | async-start | bytes 4194304 | tf_op jit(solution)/shard_map/all_to_all | solution.py:66
  167.1 0.6 bitcast_multiply_fusion
  167.8 46.7 %all-to-all-done.1 = f32[64,32,256]{2,1,0:T(8,128)} async-done(((f32[64,32,256]{2,1,0:T(8,128)}), f32[64,32,256]{2,1,0:T(8,128)}, u32[]{:S(2)}, u32[]{:S(2)}) %all-to-all-start.1) | async-done | bytes 2097184 | tf_op jit(solution)/shard_map/all_to_all | solution.py:66
  214.4 3.2 %copy.103 = f32[8,8,4,8,256]{4,3,0,2,1:T(8,128)} copy(f32[8,8,4,8,256]{4,3,2,1,0:T(8,128)} %bitcast.10) | data formatting | bytes 4194304 | tf_op jit(solution)/shard_map/all_to_all | solution.py:66
  (12 shorter events, 0.1 us)
Async XLA Ops:
  0.6 155.8 %copy-start = (f32[64,64]{1,0:T(8,128)S(1)}, f32[64,64]{1,0:T(8,128)}, u32[]{:S(2)}) copy-start(f32[64,64]{1,0:T(8,128)} %param.13) | copy-start | bytes 49156
  0.6 24.7 %copy-start.1 = (f32[8,32,2048]{2,1,0:T(8,128)S(1)}, f32[8,32,2048]{2,1,0:T(8,128)}, u32[]{:S(2)}) copy-start(f32[8,32,2048]{2,1,0:T(8,128)} %param.7) | copy-start | bytes 6291460
  2.1 3.7 %collective-permute-start = (f32[8,1,2048]{2,0,1:T(8,128)S(1)}, f32[8,1,2048]{2,0,1:T(8,128)S(1)}, u32[]{:S(2)}, u32[]{:S(2)}) collective-permute-start(f32[8,1,2048]{2,0,1:T(8,128)S(1)} %copy.101), channel_id=1, source_target_pairs={{0,8},{8,16},{16,24},{1,9},{9,17},{17,25},{2,10},{10,18},{18,26},{... | collective-permute-start | bytes 196616 | tf_op jit(solution)/shard_map/ppermute | solution.py:17
  4.5 5.3 %collective-permute-start.1 = (f32[8,1,2048]{2,0,1:T(8,128)S(1)}, f32[8,1,2048]{2,0,1:T(8,128)S(1)}, u32[]{:S(2)}, u32[]{:S(2)}) collective-permute-start(f32[8,1,2048]{2,0,1:T(8,128)S(1)} %copy.102), channel_id=1, source_target_pairs={{8,0},{16,8},{24,16},{9,1},{17,9},{25,17},{10,2},{18,10},{26,18},{... | collective-permute-start | bytes 196616 | tf_op jit(solution)/shard_map/ppermute | solution.py:19
  11.0 9.3 %collective-permute-start.2 = (f32[1,34,2048]{2,1,0:T(8,128)S(1)}, f32[1,34,2048]{2,1,0:T(8,128)S(1)}, u32[]{:S(2)}, u32[]{:S(2)}) collective-permute-start(f32[1,34,2048]{2,1,0:T(8,128)S(1)} %get-tuple-element.4), channel_id=1, source_target_pairs={{0,1},{1,2},{2,3},{3,4},{4,5},{5,6},{6,7},{8,9},{9,10},{10,11},{11... | collective-permute-start | bytes 835592 | tf_op jit(solution)/shard_map/ppermute | solution.py:17
  14.4 14.0 %copy-start.2 = (f32[8,32,2048]{2,1,0:T(8,128)S(1)}, f32[8,32,2048]{2,1,0:T(8,128)}, u32[]{:S(2)}) copy-start(f32[8,32,2048]{2,1,0:T(8,128)} %param.8) | copy-start | bytes 6291460
  14.4 14.0 %copy-start.3 = (s32[8,32,2048]{2,1,0:T(8,128)S(1)}, s32[8,32,2048]{2,1,0:T(8,128)}, u32[]{:S(2)}) copy-start(s32[8,32,2048]{2,1,0:T(8,128)} %param.11) | copy-start | bytes 6291460
  14.5 14.0 %copy-start.4 = (f32[8,32,2048]{2,1,0:T(8,128)S(1)}, f32[8,32,2048]{2,1,0:T(8,128)}, u32[]{:S(2)}) copy-start(f32[8,32,2048]{2,1,0:T(8,128)} %param.10) | copy-start | bytes 6291460
  14.5 10.9 %collective-permute-start.3 = (f32[1,34,2048]{2,1,0:T(8,128)S(1)}, f32[1,34,2048]{2,1,0:T(8,128)S(1)}, u32[]{:S(2)}, u32[]{:S(2)}) collective-permute-start(f32[1,34,2048]{2,1,0:T(8,128)S(1)} %get-tuple-element.5), channel_id=1, source_target_pairs={{1,0},{2,1},{3,2},{4,3},{5,4},{6,5},{7,6},{9,8},{10,9},{11,10},{12... | collective-permute-start | bytes 835592 | tf_op jit(solution)/shard_map/ppermute | solution.py:19
  32.9 7.6 %collective-permute-start.4 = (f32[8,1,2048]{2,0,1:T(8,128)S(1)}, f32[8,1,2048]{2,0,1:T(8,128)S(1)}, u32[]{:S(2)}, u32[]{:S(2)}) collective-permute-start(f32[8,1,2048]{2,0,1:T(8,128)S(1)} %copy.90), channel_id=1, source_target_pairs={{0,8},{8,16},{16,24},{1,9},{9,17},{17,25},{2,10},{10,18},{18,26},{... | collective-permute-start | bytes 196616 | tf_op jit(solution)/shard_map/ppermute | solution.py:17
  39.1 3.1 %collective-permute-start.5 = (f32[8,1,2048]{2,0,1:T(8,128)S(1)}, f32[8,1,2048]{2,0,1:T(8,128)S(1)}, u32[]{:S(2)}, u32[]{:S(2)}) collective-permute-start(f32[8,1,2048]{2,0,1:T(8,128)S(1)} %copy.91), channel_id=1, source_target_pairs={{8,0},{16,8},{24,16},{9,1},{17,9},{25,17},{10,2},{18,10},{26,18},{... | collective-permute-start | bytes 196616 | tf_op jit(solution)/shard_map/ppermute | solution.py:19
  42.5 10.6 %collective-permute-start.6 = (f32[1,34,2048]{2,1,0:T(8,128)S(1)}, f32[1,34,2048]{2,1,0:T(8,128)S(1)}, u32[]{:S(2)}, u32[]{:S(2)}) collective-permute-start(f32[1,34,2048]{2,1,0:T(8,128)S(1)} %get-tuple-element.2), channel_id=1, source_target_pairs={{0,1},{1,2},{2,3},{3,4},{4,5},{5,6},{6,7},{8,9},{9,10},{10,11},{11... | collective-permute-start | bytes 835592 | tf_op jit(solution)/shard_map/ppermute | solution.py:17
  46.6 14.8 %copy-start.5 = (f32[8,32,2048]{2,1,0:T(8,128)S(1)}, f32[8,32,2048]{2,1,0:T(8,128)}, u32[]{:S(2)}) copy-start(f32[8,32,2048]{2,1,0:T(8,128)} %param.9) | copy-start | bytes 6291460
  46.6 11.7 %collective-permute-start.7 = (f32[1,34,2048]{2,1,0:T(8,128)S(1)}, f32[1,34,2048]{2,1,0:T(8,128)S(1)}, u32[]{:S(2)}, u32[]{:S(2)}) collective-permute-start(f32[1,34,2048]{2,1,0:T(8,128)S(1)} %get-tuple-element.3), channel_id=1, source_target_pairs={{1,0},{2,1},{3,2},{4,3},{5,4},{6,5},{7,6},{9,8},{10,9},{11,10},{12... | collective-permute-start | bytes 835592 | tf_op jit(solution)/shard_map/ppermute | solution.py:19
  162.6 4.5 %copy-start.6 = (s32[32,256]{1,0:T(8,128)S(1)}, s32[32,256]{1,0:T(8,128)}, u32[]{:S(2)}) copy-start(s32[32,256]{1,0:T(8,128)} %param.12) | copy-start | bytes 98308
  162.6 51.8 %all-to-all-start.1 = ((f32[64,32,256]{2,1,0:T(8,128)}), f32[64,32,256]{2,1,0:T(8,128)}, u32[]{:S(2)}, u32[]{:S(2)}) async-start(f32[64,32,256]{2,1,0:T(8,128)} %copy.98), calls=%async_computation.1 | async-start | bytes 4194304 | tf_op jit(solution)/shard_map/all_to_all | solution.py:66
where the time goes:
time: 218 us
  waiting for transfers between devices  71.9 us (33%)
  blocking collectives  59.5 us (27%)
  local copies, waits for them, and re-layouts  32.9 us (15%)
  starting transfers between devices  26.2 us (12%)
  other arithmetic  22.6 us (10%)
  matrix products  3.6 us (2%)
    all_to_all x1, blocking collectives, body(): lax.all_to_all(current_tracer_values, 'tile', split_axis=2, concat_axis=0...  59.5 us
    all_to_all x1, waiting for transfers between devices, body(): lax.all_to_all(smoothed_field, 'tile', split_axis=0, concat_axis=2, tiled...  46.7 us
    ppermute x4, starting transfers between devices, with_halo(): lax.ppermute(tail, axis, [(i, (i + 1) % count) for i in range(ends)])  16.1 us
    ppermute x4, waiting for transfers between devices, with_halo(): lax.ppermute(head, axis, [((i + 1) % count, i) for i in range(ends)])  15.8 us
    unnamed x18, local copies, waits for them, and re-layouts  13.5 us
    ppermute x4, waiting for transfers between devices, with_halo(): lax.ppermute(tail, axis, [(i, (i + 1) % count) for i in range(ends)])  9.4 us
    mul x2, other arithmetic, advance(): wet_cells * (center + misfit + change + 0.1 * lateral + 0.15 * vertical)  7.31 us
    all_to_all x1, other arithmetic, body(): lax.all_to_all(current_tracer_values, 'tile', split_axis=2, concat_axis=0...  7.22 us
  transfers between devices with their start and end apart: 9, of which 7 were waited for; matrix products, arithmetic and copies ran while one was open for 0% of the time, Pallas kernels for 0%

commit v1 on v0

--- a/solution.py
+++ b/solution.py
@@ -60,7 +60,12 @@
         bordered = with_halo(current_tracer_values, (("grp", 1), ("tile", 0)), 1)
         padded = jnp.pad(bordered, ((0, 0), (0, 0), (1, 1)))
         current_tracer_values = advance(padded, misfit, east_speed, north_speed, wet_cells)
-    pencil = lax.all_to_all(current_tracer_values, "tile", split_axis=2, concat_axis=0, tiled=True)
+    pencil = jnp.concatenate(
+        lax.all_to_all(
+            jnp.stack(jnp.split(current_tracer_values, lax.axis_size("tile"), axis=2)), "tile", 0, 0
+        ),
+        axis=0,
+    )
     smoothed_field = smooth_levels(vertical_filter_matrix, pencil)
     surface_layer = smoothed_field[0]
     filtered_thermal_sensitivity = lax.all_to_all(

time: 218 us -> 185 us (0.85)
  local copies, waits for them, and re-layouts: 32.9 us -> 7.49 us
  other arithmetic: 22.6 us -> 15.4 us
    unnamed x18 -> x21, local copies, waits for them, and re-layouts: 13.5 us -> 0.18 us
    all_to_all x1 -> x0, other arithmetic: 7.22 us -> none  [body(): lax.all_to_all(current_tracer_values, 'tile', split_axis=2, concat_axis=0...]
    all_to_all x2 -> x0, local copies, waits for them, and re-layouts: 7.09 us -> none  [body(): lax.all_to_all(current_tracer_values, 'tile', split_axis=2, concat_axis=0...]
    mul x1 -> x0, local copies, waits for them, and re-layouts: 4.74 us -> none  [advance(): wet_cells * (center + misfit + change + 0.1 * lateral + 0.15 * vertical)]
where the time goes in v1:
time: 185 us
  waiting for transfers between devices  72 us (39%)
  blocking collectives  59.4 us (32%)
  starting transfers between devices  26.1 us (14%)
  other arithmetic  15.4 us (8%)
  local copies, waits for them, and re-layouts  7.49 us (4%)
  matrix products  3.26 us (2%)
    all_to_all x1, blocking collectives, body(): lax.all_to_all(jnp.stack(jnp.split(current_tracer_values, lax.axis_size('...  59.4 us
    all_to_all x1, waiting for transfers between devices, body(): lax.all_to_all(smoothed_field, 'tile', split_axis=0, concat_axis=2, tiled...  46.7 us
    ppermute x4, starting transfers between devices, with_halo(): lax.ppermute(tail, axis, [(i, (i + 1) % count) for i in range(ends)])  16.1 us
    ppermute x4, waiting for transfers between devices, with_halo(): lax.ppermute(head, axis, [((i + 1) % count, i) for i in range(ends)])  16 us
    ppermute x4, waiting for transfers between devices, with_halo(): lax.ppermute(tail, axis, [(i, (i + 1) % count) for i in range(ends)])  9.4 us
    mul x2, other arithmetic, advance(): wet_cells * (center + misfit + change + 0.1 * lateral + 0.15 * vertical)  7.31 us
    concatenate x2, other arithmetic, with_halo(): jnp.concatenate([lax.ppermute(tail, axis, [(i, (i + 1) % count) for i in...  6.23 us
    ppermute x4, starting transfers between devices, with_halo(): lax.ppermute(head, axis, [((i + 1) % count, i) for i in range(ends)])  5.56 us
  transfers between devices with their start and end apart: 9, of which 7 were waited for; matrix products, arithmetic and copies ran while one was open for 0% of the time, Pallas kernels for 0%

profile of v1, /device:TPU:0, one launch (start us, length us, event | category | flops | bytes accessed | tf_op | source)
XLA Modules:
  0.0 184.7 jit_solution(6528239351738529636)
XLA Ops:
  0.6 0.0 copy-start
  0.6 0.0 copy-start.1
  0.7 1.4 fusion.27
  2.1 2.4 %collective-permute-start = (f32[8,1,2048]{2,1,0:T(1,128)S(1)}, f32[8,1,2048]{2,1,0:T(1,128)S(1)}, u32[]{:S(2)}, u32[]{:S(2)}) collective-permute-start(f32[8,1,2048]{2,1,0:T(1,128)S(1)} %get-tuple-element.8), channel_id=1, source_target_pairs={{0,8},{8,16},{16,24},{1,9},{9,17},{17,25},{2,10},{10,18},{18,26},{... | collective-permute-start | bytes 196616 | tf_op jit(solution)/shard_map/ppermute | solution.py:17
  4.5 1.3 collective-permute-start.1
  5.8 0.0 collective-permute-done
  5.8 4.0 %collective-permute-done.1 = f32[8,1,2048]{2,1,0:T(1,128)S(1)} collective-permute-done((f32[8,1,2048]{2,1,0:T(1,128)S(1)}, f32[8,1,2048]{2,1,0:T(1,128)S(1)}, u32[]{:S(2)}, u32[]{:S(2)}) %collective-permute-start.1) | collective-permute-done | bytes 65568 | tf_op jit(solution)/shard_map/ppermute | solution.py:19
  9.8 1.1 pad_maximum_fusion.21
  10.9 3.4 %collective-permute-start.2 = (f32[1,34,2048]{2,1,0:T(8,128)S(1)}, f32[1,34,2048]{2,1,0:T(8,128)S(1)}, u32[]{:S(2)}, u32[]{:S(2)}) collective-permute-start(f32[1,34,2048]{2,1,0:T(8,128)S(1)} %get-tuple-element.4), channel_id=1, source_target_pairs={{0,1},{1,2},{2,3},{3,4},{4,5},{5,6},{6,7},{8,9},{9,10},{10,11},{11... | collective-permute-start | bytes 835592 | tf_op jit(solution)/shard_map/ppermute | solution.py:17
  14.3 0.0 copy-start.2
  14.3 0.0 copy-start.3
  14.3 0.0 copy-start.4
  14.3 1.6 collective-permute-start.3
  15.9 4.3 %collective-permute-done.2 = f32[1,34,2048]{2,1,0:T(8,128)S(1)} collective-permute-done((f32[1,34,2048]{2,1,0:T(8,128)S(1)}, f32[1,34,2048]{2,1,0:T(8,128)S(1)}, u32[]{:S(2)}, u32[]{:S(2)}) %collective-permute-start.2) | collective-permute-done | bytes 278560 | tf_op jit(solution)/shard_map/ppermute | solution.py:17
  20.2 5.0 %collective-permute-done.3 = f32[1,34,2048]{2,1,0:T(8,128)S(1)} collective-permute-done((f32[1,34,2048]{2,1,0:T(8,128)S(1)}, f32[1,34,2048]{2,1,0:T(8,128)S(1)}, u32[]{:S(2)}, u32[]{:S(2)}) %collective-permute-start.3) | collective-permute-done | bytes 278560 | tf_op jit(solution)/shard_map/ppermute | solution.py:19
  25.2 0.0 copy-done.1
  25.2 3.1 %select_maximum_fusion.4 = f32[10,34,2050]{2,1,0:T(8,128)S(1)} fusion(f32[1,34,2048]{2,1,0:T(8,128)S(1)} %collective-permute-done.3, f32[1,34,2048]{2,1,0:T(8,128)S(1)} %collective-permute-done.2, f32[8,1,2048]{2,1,0:T(1,128)S(1)} %collective-permute-done.1, f32[8,32,2048]{2,1,0:T(8,128)S(1)} %copy-done.1, f32[8,1,2048]{2,1,0:T(1,128)S(1)} %collective-permute-done), kind=kLoop, calls=%fused_computation.6 | loop fusion | flops 8364000 | bytes 5573280 | tf_op jit(solution)/shard_map/concatenate | solution.py:15
  28.3 0.0 copy-done.2
  28.3 0.0 copy-done.3
  28.3 0.0 copy-done.4
  28.3 4.3 %fusion.10 = f32[8,32,2048]{2,1,0:T(8,128)S(1)} fusion(f32[1,34,2048]{2,1,0:T(8,128)S(1)} %collective-permute-done.3, f32[8,1,2048]{2,1,0:T(1,128)S(1)} %collective-permute-done.1, f32[8,32,2048]{2,1,0:T(8,128)S(1)} %copy-done.1, f32[8,1,2048]{2,1,0:T(1,128)S(1)} %collective-permute-done, f32[1,34,2048]{2,1,0:T(8,128)S(1)} %collective-permute-done.2, ...), kind=kLoop, calls=%fused_computation.29 | loop fusion | flops 16252928 | bytes 17465344 | tf_op jit(solution)/shard_map/mul | solution.py:39
  32.6 0.1 fusion.26
  32.7 6.2 %collective-permute-start.4 = (f32[8,1,2048]{2,1,0:T(1,128)S(1)}, f32[8,1,2048]{2,1,0:T(1,128)S(1)}, u32[]{:S(2)}, u32[]{:S(2)}) collective-permute-start(f32[8,1,2048]{2,1,0:T(1,128)S(1)} %get-tuple-element.6), channel_id=1, source_target_pairs={{0,8},{8,16},{16,24},{1,9},{9,17},{17,25},{2,10},{10,18},{18,26},{... | collective-permute-start | bytes 196616 | tf_op jit(solution)/shard_map/ppermute | solution.py:17
  38.9 1.3 collective-permute-start.5
  40.2 0.0 collective-permute-done.4
  40.3 1.8 collective-permute-done.5
  42.1 0.1 pad_maximum_fusion.18
  42.2 4.1 %collective-permute-start.6 = (f32[1,34,2048]{2,1,0:T(8,128)S(1)}, f32[1,34,2048]{2,1,0:T(8,128)S(1)}, u32[]{:S(2)}, u32[]{:S(2)}) collective-permute-start(f32[1,34,2048]{2,1,0:T(8,128)S(1)} %get-tuple-element.2), channel_id=1, source_target_pairs={{0,1},{1,2},{2,3},{3,4},{4,5},{5,6},{6,7},{8,9},{9,10},{10,11},{11... | collective-permute-start | bytes 835592 | tf_op jit(solution)/shard_map/ppermute | solution.py:17
  46.3 0.0 copy-start.5
  46.3 1.4 collective-permute-start.7
  47.7 5.1 %collective-permute-done.6 = f32[1,34,2048]{2,1,0:T(8,128)S(1)} collective-permute-done((f32[1,34,2048]{2,1,0:T(8,128)S(1)}, f32[1,34,2048]{2,1,0:T(8,128)S(1)}, u32[]{:S(2)}, u32[]{:S(2)}) %collective-permute-start.6) | collective-permute-done | bytes 278560 | tf_op jit(solution)/shard_map/ppermute | solution.py:17
  52.8 5.2 %collective-permute-done.7 = f32[1,34,2048]{2,1,0:T(8,128)S(1)} collective-permute-done((f32[1,34,2048]{2,1,0:T(8,128)S(1)}, f32[1,34,2048]{2,1,0:T(8,128)S(1)}, u32[]{:S(2)}, u32[]{:S(2)}) %collective-permute-start.7) | collective-permute-done | bytes 278560 | tf_op jit(solution)/shard_map/ppermute | solution.py:19
  58.0 3.1 %select_maximum_fusion = f32[10,34,2050]{2,1,0:T(8,128)S(1)} fusion(f32[1,34,2048]{2,1,0:T(8,128)S(1)} %collective-permute-done.7, f32[1,34,2048]{2,1,0:T(8,128)S(1)} %collective-permute-done.6, f32[8,1,2048]{2,1,0:T(1,128)S(1)} %collective-permute-done.5, f32[8,32,2048]{2,1,0:T(8,128)S(1)} %fusion.10, f32[8,1,2048]{2,1,0:T(1,128)S(1)} %collective-permute-done.4), kind=kLoop, calls=%fused_computation.2 | loop fusion | flops 8364000 | bytes 5573280 | tf_op jit(solution)/shard_map/concatenate | solution.py:15
  61.1 0.0 copy-done.5
  61.1 3.0 %fusion.5 = f32[8,32,2048]{2,1,0:T(8,128)S(1)} fusion(f32[1,34,2048]{2,1,0:T(8,128)S(1)} %collective-permute-done.7, f32[8,1,2048]{2,1,0:T(1,128)S(1)} %collective-permute-done.5, f32[8,32,2048]{2,1,0:T(8,128)S(1)} %fusion.10, f32[8,1,2048]{2,1,0:T(1,128)S(1)} %collective-permute-done.4, f32[1,34,2048]{2,1,0:T(8,128)S(1)} %collective-permute-done.6, ...), kind=kLoop, calls=%fused_computation.16 | loop fusion | flops 16252928 | bytes 17465344 | tf_op jit(solution)/shard_map/mul | solution.py:39
  64.4 59.4 %all_to_all.23 = f32[8,8,32,256]{3,2,1,0:T(8,128)S(1)} all-to-all(f32[8,8,32,256]{3,2,1,0:T(8,128)S(1)} %fusion.17), channel_id=1, replica_groups=mesh['grp'=4,'tile'=8] {'tile'}, dimensions={0} | all-to-all | bytes 4194304 | tf_op jit(solution)/shard_map/all_to_all | solution.py:64
  123.8 0.0 copy-done
  123.8 3.3 %fusion.14 = f32[64,32,256]{2,0,1:T(8,128)S(1)} fusion(f32[8,8,32,256]{3,2,1,0:T(8,128)S(1)} %all_to_all.23, f32[64,64]{1,0:T(8,128)S(1)} %copy-done), kind=kOutput, calls=%fused_computation.40 | convolution fusion | flops 402653184 | bytes 4210688 | tf_op jit(solution)/shard_map/cz,zne->cne/dot_general | solution.py:43
  127.1 2.5 %copy.12 = f32[64,32,256]{2,1,0:T(8,128)} copy(f32[64,32,256]{2,0,1:T(8,128)S(1)} %fusion.14) | data formatting | bytes 4194304 | tf_op jit(solution)/shard_map/cz,zne->cne/dot_general | solution.py:43
  129.6 0.0 copy-start.6
  129.6 4.5 %all-to-all-start.1 = ((f32[64,32,256]{2,1,0:T(8,128)}), f32[64,32,256]{2,1,0:T(8,128)}, u32[]{:S(2)}, u32[]{:S(2)}) async-start(f32[64,32,256]{2,1,0:T(8,128)} %copy.12), calls=%async_computation.1 | async-start | bytes 4194304 | tf_op jit(solution)/shard_map/all_to_all | solution.py:71
  134.2 0.0 copy-done.6
  134.2 0.6 bitcast_multiply_fusion
  134.8 46.7 %all-to-all-done.1 = f32[64,32,256]{2,1,0:T(8,128)} async-done(((f32[64,32,256]{2,1,0:T(8,128)}), f32[64,32,256]{2,1,0:T(8,128)}, u32[]{:S(2)}, u32[]{:S(2)}) %all-to-all-start.1) | async-done | bytes 2097184 | tf_op jit(solution)/shard_map/all_to_all | solution.py:71
  181.5 3.2 %copy.15 = f32[8,8,4,8,256]{4,3,0,2,1:T(8,128)} copy(f32[8,8,4,8,256]{4,3,2,1,0:T(8,128)} %bitcast.15) | data formatting | bytes 4194304 | tf_op jit(solution)/shard_map/all_to_all | solution.py:71
  (9 shorter events, 0.2 us)
Async XLA Ops:
  0.6 123.2 %copy-start = (f32[64,64]{1,0:T(8,128)S(1)}, f32[64,64]{1,0:T(8,128)}, u32[]{:S(2)}) copy-start(f32[64,64]{1,0:T(8,128)} %param.13) | copy-start | bytes 49156
  0.6 24.6 %copy-start.1 = (f32[8,32,2048]{2,1,0:T(8,128)S(1)}, f32[8,32,2048]{2,1,0:T(8,128)}, u32[]{:S(2)}) copy-start(f32[8,32,2048]{2,1,0:T(8,128)} %param.7) | copy-start | bytes 6291460
  2.1 3.7 %collective-permute-start = (f32[8,1,2048]{2,1,0:T(1,128)S(1)}, f32[8,1,2048]{2,1,0:T(1,128)S(1)}, u32[]{:S(2)}, u32[]{:S(2)}) collective-permute-start(f32[8,1,2048]{2,1,0:T(1,128)S(1)} %get-tuple-element.8), channel_id=1, source_target_pairs={{0,8},{8,16},{16,24},{1,9},{9,17},{17,25},{2,10},{10,18},{18,26},{... | collective-permute-start | bytes 196616 | tf_op jit(solution)/shard_map/ppermute | solution.py:17
  4.5 5.3 %collective-permute-start.1 = (f32[8,1,2048]{2,1,0:T(1,128)S(1)}, f32[8,1,2048]{2,1,0:T(1,128)S(1)}, u32[]{:S(2)}, u32[]{:S(2)}) collective-permute-start(f32[8,1,2048]{2,1,0:T(1,128)S(1)} %get-tuple-element.9), channel_id=1, source_target_pairs={{8,0},{16,8},{24,16},{9,1},{17,9},{25,17},{10,2},{18,10},{26,18},{... | collective-permute-start | bytes 196616 | tf_op jit(solution)/shard_map/ppermute | solution.py:19
  10.9 9.3 %collective-permute-start.2 = (f32[1,34,2048]{2,1,0:T(8,128)S(1)}, f32[1,34,2048]{2,1,0:T(8,128)S(1)}, u32[]{:S(2)}, u32[]{:S(2)}) collective-permute-start(f32[1,34,2048]{2,1,0:T(8,128)S(1)} %get-tuple-element.4), channel_id=1, source_target_pairs={{0,1},{1,2},{2,3},{3,4},{4,5},{5,6},{6,7},{8,9},{9,10},{10,11},{11... | collective-permute-start | bytes 835592 | tf_op jit(solution)/shard_map/ppermute | solution.py:17
  14.3 14.0 %copy-start.2 = (f32[8,32,2048]{2,1,0:T(8,128)S(1)}, f32[8,32,2048]{2,1,0:T(8,128)}, u32[]{:S(2)}) copy-start(f32[8,32,2048]{2,1,0:T(8,128)} %param.8) | copy-start | bytes 6291460
  14.3 14.0 %copy-start.3 = (s32[8,32,2048]{2,1,0:T(8,128)S(1)}, s32[8,32,2048]{2,1,0:T(8,128)}, u32[]{:S(2)}) copy-start(s32[8,32,2048]{2,1,0:T(8,128)} %param.11) | copy-start | bytes 6291460
  14.3 14.0 %copy-start.4 = (f32[8,32,2048]{2,1,0:T(8,128)S(1)}, f32[8,32,2048]{2,1,0:T(8,128)}, u32[]{:S(2)}) copy-start(f32[8,32,2048]{2,1,0:T(8,128)} %param.10) | copy-start | bytes 6291460
  14.3 10.9 %collective-permute-start.3 = (f32[1,34,2048]{2,1,0:T(8,128)S(1)}, f32[1,34,2048]{2,1,0:T(8,128)S(1)}, u32[]{:S(2)}, u32[]{:S(2)}) collective-permute-start(f32[1,34,2048]{2,1,0:T(8,128)S(1)} %get-tuple-element.5), channel_id=1, source_target_pairs={{1,0},{2,1},{3,2},{4,3},{5,4},{6,5},{7,6},{9,8},{10,9},{11,10},{12... | collective-permute-start | bytes 835592 | tf_op jit(solution)/shard_map/ppermute | solution.py:19
  32.7 7.5 %collective-permute-start.4 = (f32[8,1,2048]{2,1,0:T(1,128)S(1)}, f32[8,1,2048]{2,1,0:T(1,128)S(1)}, u32[]{:S(2)}, u32[]{:S(2)}) collective-permute-start(f32[8,1,2048]{2,1,0:T(1,128)S(1)} %get-tuple-element.6), channel_id=1, source_target_pairs={{0,8},{8,16},{16,24},{1,9},{9,17},{17,25},{2,10},{10,18},{18,26},{... | collective-permute-start | bytes 196616 | tf_op jit(solution)/shard_map/ppermute | solution.py:17
  38.9 3.1 %collective-permute-start.5 = (f32[8,1,2048]{2,1,0:T(1,128)S(1)}, f32[8,1,2048]{2,1,0:T(1,128)S(1)}, u32[]{:S(2)}, u32[]{:S(2)}) collective-permute-start(f32[8,1,2048]{2,1,0:T(1,128)S(1)} %get-tuple-element.7), channel_id=1, source_target_pairs={{8,0},{16,8},{24,16},{9,1},{17,9},{25,17},{10,2},{18,10},{26,18},{... | collective-permute-start | bytes 196616 | tf_op jit(solution)/shard_map/ppermute | solution.py:19
  42.2 10.6 %collective-permute-start.6 = (f32[1,34,2048]{2,1,0:T(8,128)S(1)}, f32[1,34,2048]{2,1,0:T(8,128)S(1)}, u32[]{:S(2)}, u32[]{:S(2)}) collective-permute-start(f32[1,34,2048]{2,1,0:T(8,128)S(1)} %get-tuple-element.2), channel_id=1, source_target_pairs={{0,1},{1,2},{2,3},{3,4},{4,5},{5,6},{6,7},{8,9},{9,10},{10,11},{11... | collective-permute-start | bytes 835592 | tf_op jit(solution)/shard_map/ppermute | solution.py:17
  46.3 14.8 %copy-start.5 = (f32[8,32,2048]{2,1,0:T(8,128)S(1)}, f32[8,32,2048]{2,1,0:T(8,128)}, u32[]{:S(2)}) copy-start(f32[8,32,2048]{2,1,0:T(8,128)} %param.9) | copy-start | bytes 6291460
  46.3 11.7 %collective-permute-start.7 = (f32[1,34,2048]{2,1,0:T(8,128)S(1)}, f32[1,34,2048]{2,1,0:T(8,128)S(1)}, u32[]{:S(2)}, u32[]{:S(2)}) collective-permute-start(f32[1,34,2048]{2,1,0:T(8,128)S(1)} %get-tuple-element.3), channel_id=1, source_target_pairs={{1,0},{2,1},{3,2},{4,3},{5,4},{6,5},{7,6},{9,8},{10,9},{11,10},{12... | collective-permute-start | bytes 835592 | tf_op jit(solution)/shard_map/ppermute | solution.py:19
  129.6 4.5 %copy-start.6 = (s32[32,256]{1,0:T(8,128)S(1)}, s32[32,256]{1,0:T(8,128)}, u32[]{:S(2)}) copy-start(s32[32,256]{1,0:T(8,128)} %param.12) | copy-start | bytes 98308
  129.6 51.8 %all-to-all-start.1 = ((f32[64,32,256]{2,1,0:T(8,128)}), f32[64,32,256]{2,1,0:T(8,128)}, u32[]{:S(2)}, u32[]{:S(2)}) async-start(f32[64,32,256]{2,1,0:T(8,128)} %copy.12), calls=%async_computation.1 | async-start | bytes 4194304 | tf_op jit(solution)/shard_map/all_to_all | solution.py:71
